TPU v7x, 32 devices: a whole 2x2x4 slice. The times are simulated.
32 devices in a mesh: freq: 4 (over y, core), gx: 8 (over z, x).
Axes of the slice: x: 2, y: 2, z: 4, core: 2. Of those that a mesh axis runs over, the one named last changes fastest.
Arguments:
- sigma_h: float32 [32, 64, 256], P('gx'), may hold values from 0.3 to 3
- sigma_v: float32 [32, 64, 256], P('gx'), may hold values from 0.3 to 3
- wave_scale: float32 [4], P('freq'), may hold values from 0.25 to 4
- field_start: bfloat16 [4, 2, 3, 32, 64, 256], P('freq', None, None, 'gx'), may hold values from -6 to 6
- adjoint_start: bfloat16 [4, 2, 3, 32, 64, 256], P('freq', None, None, 'gx'), may hold values from -6 to 6
- observed: bfloat16 [4, 2, 3, 32, 64, 256], P('freq', None, None, 'gx'), may hold values from -6 to 6
- tx_count: int32 [1], replicated, may hold values from 1 to 64
- tx_cells: int32 [64], replicated, may hold values from 0 to 524287
Outputs:
- gradient: float32 [2, 32, 64, 256], P(None, 'gx', 'freq')
- final_field: float32 [4, 2, 3, 32, 64, 256], P('freq', None, None, 'gx')
All inputs are finite; a program needn't handle non-finite values.
Results may differ from a plain program's by a relative error of at most 0.0003.
Values sent between devices are 32-bit elements; how exact they have to be, the bound alone decides.
A program may use at most 64 MiB of HBM per device.

v0:
```python
import jax
import jax.numpy as jnp
from jax import lax
from jax.sharding import PartitionSpec as P

ITERS = 2


THETA = 0.5
SOURCE_GAIN = 8.0


def padded_2(cells, sides, width):
    for axis, dim in sides:
        count = lax.axis_size(axis)
        ends = count - 1
        head = lax.slice_in_dim(cells, 0, width, axis=dim)
        tail = lax.slice_in_dim(cells, cells.shape[dim] - width, cells.shape[dim], axis=dim)
        cells = jnp.concatenate(
            [
                lax.ppermute(tail, axis, [(i, (i + 1) % count) for i in range(ends)]),
                cells,
                lax.ppermute(head, axis, [((i + 1) % count, i) for i in range(ends)]),
            ],
            axis=dim,
        )
    return cells


def ahead_diff(values, along):
    along = values.ndim + along
    widths = [(0, 0)] * values.ndim
    widths[along] = (0, 1)
    padded = jnp.pad(values, widths)
    return lax.slice_in_dim(padded, 1, values.shape[along] + 1, axis=along) - values


def behind_diff(values, along):
    along = values.ndim + along
    widths = [(0, 0)] * values.ndim
    widths[along] = (1, 0)
    padded = jnp.pad(values, widths)
    return values - lax.slice_in_dim(padded, 0, values.shape[along], axis=along)


def curl_masked(efield, inside):
    comp_x = efield[..., 0, :, :, :]
    comp_y = efield[..., 1, :, :, :]
    comp_z = efield[..., 2, :, :, :]
    twist_x = (ahead_diff(comp_z, -2) - ahead_diff(comp_y, -1)) * inside
    twist_y = (ahead_diff(comp_x, -1) - ahead_diff(comp_z, -3)) * inside
    twist_z = (ahead_diff(comp_y, -3) - ahead_diff(comp_x, -2)) * inside
    back_x = behind_diff(twist_z, -2) - behind_diff(twist_y, -1)
    back_y = behind_diff(twist_x, -1) - behind_diff(twist_z, -3)
    back_z = behind_diff(twist_y, -3) - behind_diff(twist_x, -2)
    return jnp.stack([back_x, back_y, back_z], axis=-4)


def relax(efield, curled, source_term, sig_pair, wave_scale):
    sigma_comp = jnp.stack([sig_pair[0], sig_pair[0], sig_pair[1]])
    coupling = wave_scale[:, None, None, None, None] * sigma_comp[None]
    real_part = efield[:, 0]
    imag_part = efield[:, 1]
    resid_real = source_term[:, 0] - (curled[:, 0] - coupling * imag_part)
    resid_imag = source_term[:, 1] - (curled[:, 1] + coupling * real_part)
    modulus = 16.0 + coupling * coupling
    update_real = (4.0 * resid_real + coupling * resid_imag) / modulus
    update_imag = (4.0 * resid_imag - coupling * resid_real) / modulus
    return efield + THETA * jnp.stack([update_real, update_imag], axis=1)


def make_source(tx_cells, tx_count, wave_scale, x_start, slab_width, size_y, size_z):
    plane_size = size_y * size_z
    cell_x = tx_cells // plane_size - x_start
    remainder = tx_cells % plane_size
    cell_y = remainder // size_z
    cell_z = remainder % size_z
    active = (jnp.arange(tx_cells.shape[0]) < tx_count[0]) & (cell_x >= 0) & (cell_x < slab_width)
    weights = jnp.where(active, 1.0, 0.0).astype(jnp.float32)
    counts = jnp.zeros((slab_width, size_y, size_z), jnp.float32)
    counts = counts.at[jnp.clip(cell_x, 0, slab_width - 1), cell_y, cell_z].add(weights)
    imag_x = SOURCE_GAIN * wave_scale[:, None, None, None] * counts[None]
    blank = jnp.zeros_like(imag_x)
    real_block = jnp.stack([blank, blank, blank], axis=1)
    imag_block = jnp.stack([imag_x, blank, blank], axis=1)
    return jnp.stack([real_block, imag_block], axis=1)


def adjoint_source(efield, observed):
    differ = efield - observed.astype(jnp.float32)
    return jnp.stack([differ[:, 0], -differ[:, 1]], axis=1)


def gradient_terms(efield, adjoint, wave_scale):
    product = adjoint[:, 0] * efield[:, 1] + adjoint[:, 1] * efield[:, 0]
    weighted = wave_scale[:, None, None, None, None] * product
    horizontal = jnp.sum(weighted[:, 0] + weighted[:, 1], axis=0)
    vertical = jnp.sum(weighted[:, 2], axis=0)
    return jnp.stack([horizontal, vertical])


def inside_mask(first, width, total_x):
    positions = first + jnp.arange(width)
    return ((positions >= 0) & (positions < total_x)).astype(jnp.float32)[:, None, None]


def local_sweep(efield, source_term, sig_pair, wave_scale, inside_pad):
    padded = padded_2(efield, (("gx", 3),), 1)
    curled = curl_masked(padded, inside_pad)[:, :, :, 1:-1]
    return relax(efield, curled, source_term, sig_pair, wave_scale)


def on_device(
    sigma_h, sigma_v, wave_scale, field_start, adjoint_start, observed, tx_count, tx_cells
):
    slab_width = sigma_h.shape[0]
    size_y = sigma_h.shape[1]
    size_z = sigma_h.shape[2]
    slab_index = lax.axis_index("gx")
    total_x = slab_width * lax.axis_size("gx")
    slab_first = slab_index * slab_width
    sig_pair = jnp.stack([sigma_h, sigma_v])
    efield = field_start.astype(jnp.float32)
    adjoint = adjoint_start.astype(jnp.float32)
    inside_pad = inside_mask(slab_first - 1, slab_width + 2, total_x)
    source_term = make_source(
        tx_cells, tx_count, wave_scale, slab_first, slab_width, size_y, size_z
    )
    for sweep in range(ITERS):
        efield = local_sweep(efield, source_term, sig_pair, wave_scale, inside_pad)
    adjoint_rhs = adjoint_source(efield, observed)
    for sweep in range(ITERS):
        adjoint = local_sweep(adjoint, adjoint_rhs, sig_pair, wave_scale, inside_pad)
    local_grad = gradient_terms(efield, adjoint, wave_scale)
    summed = lax.psum(local_grad, "freq")
    share_rows = size_y // lax.axis_size("freq")
    gradient = lax.dynamic_slice_in_dim(summed, lax.axis_index("freq") * share_rows, share_rows, 2)
    return (gradient, efield)


def solution(mesh):
    placed = (
        P("gx", None, None),
        P("gx", None, None),
        P("freq"),
        P("freq", None, None, "gx", None, None),
        P("freq", None, None, "gx", None, None),
        P("freq", None, None, "gx", None, None),
        P(),
        P(),
    )
    return jax.shard_map(
        on_device,
        mesh=mesh,
        in_specs=placed,
        out_specs=(P(None, "gx", "freq", None), P("freq", None, None, "gx", None, None)),
        check_vma=False,
    )
```

profile of v0, /device:TPU:8, one launch (start us, length us, event | category | flops | bytes accessed | tf_op | source)
XLA Modules:
  0.0 140.6 jit_solution(16279247246572312704)
XLA Ops:
  7.2 1.2 fusion.149
  8.4 0.8 copy.50
  9.2 3.4 %collective-permute-start = (f32[1,2,3,1,64,256]{5,4,3,1,2,0:T(8,128)}, f32[1,2,3,1,64,256]{5,4,3,1,2,0:T(8,128)}, u32[]{:S(2)}, u32[]{:S(2)}) collective-permute-start(f32[1,2,3,1,64,256]{5,4,3,1,2,0:T(8,128)} %copy.50), channel_id=1, source_target_pairs={{0,1},{1,2},{2,3},{3,4},{4,5},{5,6},{6,7},{8,9},{9,10},{10,11},{11... | collective-permute-start | bytes 1179656 | tf_op jit(solution)/shard_map/ppermute | solution.py:21
  12.5 0.8 copy.51
  13.4 3.5 %collective-permute-start.1 = (f32[1,2,3,1,64,256]{5,4,3,1,2,0:T(8,128)}, f32[1,2,3,1,64,256]{5,4,3,1,2,0:T(8,128)}, u32[]{:S(2)}, u32[]{:S(2)}) collective-permute-start(f32[1,2,3,1,64,256]{5,4,3,1,2,0:T(8,128)} %copy.51), channel_id=1, source_target_pairs={{1,0},{2,1},{3,2},{4,3},{5,4},{6,5},{7,6},{9,8},{10,9},{11,10},{12... | collective-permute-start | bytes 1179656 | tf_op jit(solution)/shard_map/ppermute | solution.py:23
  17.0 1.0 fusion.147
  18.0 2.5 %collective-permute-start.4 = (f32[1,2,3,1,64,256]{5,4,3,1,2,0:T(8,128)}, f32[1,2,3,1,64,256]{5,4,3,1,2,0:T(8,128)}, u32[]{:S(2)}, u32[]{:S(2)}) collective-permute-start(f32[1,2,3,1,64,256]{5,4,3,1,2,0:T(8,128)} %get-tuple-element.30), channel_id=1, source_target_pairs={{0,1},{1,2},{2,3},{3,4},{4,5},{5,6},{6,7},{8,9},{9,10},{10,11},{11... | collective-permute-start | bytes 1179656 | tf_op jit(solution)/shard_map/ppermute | solution.py:21
  20.5 4.2 %collective-permute-start.5 = (f32[1,2,3,1,64,256]{5,4,3,1,2,0:T(8,128)}, f32[1,2,3,1,64,256]{5,4,3,1,2,0:T(8,128)}, u32[]{:S(2)}, u32[]{:S(2)}) collective-permute-start(f32[1,2,3,1,64,256]{5,4,3,1,2,0:T(8,128)} %get-tuple-element.31), channel_id=1, source_target_pairs={{1,0},{2,1},{3,2},{4,3},{5,4},{6,5},{7,6},{9,8},{10,9},{11,10},{12... | collective-permute-start | bytes 1179656 | tf_op jit(solution)/shard_map/ppermute | solution.py:23
  25.5 1.3 convert_element_type.71
  27.5 4.6 %scatter_fusion = f32[4,64,256]{2,1,0:T(8,128)S(1)} fusion(f32[4,64,256]{2,1,0:T(8,128)S(1)} %broadcast_in_dim.16, s32[64]{0:T(128)S(1)} %fusion.137, f32[64]{0:T(128)S(1)} %get-tuple-element.14), kind=kCustom, calls=%fused_computation | custom fusion | flops 64 | bytes 1536 | tf_op jit(solution)/shard_map/scatter-add | solution.py:81
  32.1 7.1 %collective-permute-done = f32[1,2,3,1,64,256]{5,4,3,1,2,0:T(8,128)} collective-permute-done((f32[1,2,3,1,64,256]{5,4,3,1,2,0:T(8,128)}, f32[1,2,3,1,64,256]{5,4,3,1,2,0:T(8,128)}, u32[]{:S(2)}, u32[]{:S(2)}) %collective-permute-start) | collective-permute-done | bytes 393248 | tf_op jit(solution)/shard_map/ppermute | solution.py:21
  39.2 1.0 constant_dynamic-update-slice_fusion.2
  40.4 1.0 constant_dynamic-update-slice_fusion
  41.6 0.6 fusion.6
  42.3 0.6 fusion.9
  43.3 0.6 copy-done.4
  44.9 4.4 %collective-permute-start.2 = (f32[1,2,3,1,64,256]{5,4,3,1,2,0:T(8,128)S(1)}, f32[1,2,3,1,64,256]{5,4,3,1,2,0:T(8,128)S(1)}, u32[]{:S(2)}, u32[]{:S(2)}) collective-permute-start(f32[1,2,3,1,64,256]{5,4,3,1,2,0:T(8,128)S(1)} %copy.52), channel_id=1, source_target_pairs={{0,1},{1,2},{2,3},{3,4},{4,5},{5,6},{6,7},{8,9},{9,10},{10,11},{11... | collective-permute-start | bytes 1179656 | tf_op jit(solution)/shard_map/ppermute | solution.py:21
  49.3 2.4 %collective-permute-start.3 = (f32[1,2,3,1,64,256]{5,4,3,1,2,0:T(8,128)S(1)}, f32[1,2,3,1,64,256]{5,4,3,1,2,0:T(8,128)S(1)}, u32[]{:S(2)}, u32[]{:S(2)}) collective-permute-start(f32[1,2,3,1,64,256]{5,4,3,1,2,0:T(8,128)S(1)} %copy.53), channel_id=1, source_target_pairs={{1,0},{2,1},{3,2},{4,3},{5,4},{6,5},{7,6},{9,8},{10,9},{11,10},{12... | collective-permute-start | bytes 1179656 | tf_op jit(solution)/shard_map/ppermute | solution.py:23
  51.7 1.4 pad_maximum_fusion
  53.3 10.7 %collective-permute-done.2 = f32[1,2,3,1,64,256]{5,4,3,1,2,0:T(8,128)S(1)} collective-permute-done((f32[1,2,3,1,64,256]{5,4,3,1,2,0:T(8,128)S(1)}, f32[1,2,3,1,64,256]{5,4,3,1,2,0:T(8,128)S(1)}, u32[]{:S(2)}, u32[]{:S(2)}) %collective-permute-start.2) | collective-permute-done | bytes 393248 | tf_op jit(solution)/shard_map/ppermute | solution.py:21
  64.3 2.3 %collective-permute-done.3 = f32[1,2,3,1,64,256]{5,4,3,1,2,0:T(8,128)S(1)} collective-permute-done((f32[1,2,3,1,64,256]{5,4,3,1,2,0:T(8,128)S(1)}, f32[1,2,3,1,64,256]{5,4,3,1,2,0:T(8,128)S(1)}, u32[]{:S(2)}, u32[]{:S(2)}) %collective-permute-start.3) | collective-permute-done | bytes 393248 | tf_op jit(solution)/shard_map/ppermute | solution.py:23
  66.9 1.5 %fusion.30 = (f32[1,2,6,64,256]{4,3,2,1,0:T(8,128)S(1)}, f32[1,2,6,64,256]{4,3,2,1,0:T(8,128)S(1)}, f32[1,2,6,64,256]{4,3,2,1,0:T(8,128)S(1)}, f32[1,2,6,64,256]...) fusion(f32[1,2,6,64,256]{4,3,2,1,0:T(8,128)S(1)} %get-tuple-element.19, ...), kind=kLoop, calls=%fused_computation.89 | loop fusion | flops 4718592 | bytes 9437208 | tf_op jit(solution)/shard_map/mul | solution.py:52
  70.2 0.9 copy-done.6
  72.5 2.1 %collective-permute-start.6 = (f32[1,2,3,1,64,256]{5,4,3,1,2,0:T(8,128)S(1)}, f32[1,2,3,1,64,256]{5,4,3,1,2,0:T(8,128)S(1)}, u32[]{:S(2)}, u32[]{:S(2)}) collective-permute-start(f32[1,2,3,1,64,256]{5,4,3,1,2,0:T(8,128)S(1)} %get-tuple-element.29), channel_id=1, source_target_pairs={{0,1},{1,2},{2,3},{3,4},{4,5},{5,6},{6,7},{8,9},{9,10},{10,11},{11... | collective-permute-start | bytes 1179656 | tf_op jit(solution)/shard_map/ppermute | solution.py:21
  75.0 4.8 %collective-permute-start.7 = (f32[1,2,3,1,64,256]{5,4,3,1,2,0:T(8,128)S(1)}, f32[1,2,3,1,64,256]{5,4,3,1,2,0:T(8,128)S(1)}, u32[]{:S(2)}, u32[]{:S(2)}) collective-permute-start(f32[1,2,3,1,64,256]{5,4,3,1,2,0:T(8,128)S(1)} %get-tuple-element.28), channel_id=1, source_target_pairs={{1,0},{2,1},{3,2},{4,3},{5,4},{6,5},{7,6},{9,8},{10,9},{11,10},{12... | collective-permute-start | bytes 1179656 | tf_op jit(solution)/shard_map/ppermute | solution.py:23
  80.2 11.5 %collective-permute-done.6 = f32[1,2,3,1,64,256]{5,4,3,1,2,0:T(8,128)S(1)} collective-permute-done((f32[1,2,3,1,64,256]{5,4,3,1,2,0:T(8,128)S(1)}, f32[1,2,3,1,64,256]{5,4,3,1,2,0:T(8,128)S(1)}, u32[]{:S(2)}, u32[]{:S(2)}) %collective-permute-start.6) | collective-permute-done | bytes 393248 | tf_op jit(solution)/shard_map/ppermute | solution.py:21
  91.9 2.8 %collective-permute-done.7 = f32[1,2,3,1,64,256]{5,4,3,1,2,0:T(8,128)S(1)} collective-permute-done((f32[1,2,3,1,64,256]{5,4,3,1,2,0:T(8,128)S(1)}, f32[1,2,3,1,64,256]{5,4,3,1,2,0:T(8,128)S(1)}, u32[]{:S(2)}, u32[]{:S(2)}) %collective-permute-start.7) | collective-permute-done | bytes 393248 | tf_op jit(solution)/shard_map/ppermute | solution.py:23
  94.9 0.7 fusion.42
  96.2 0.6 add_divide_fusion
  97.7 0.8 pad_maximum_fusion.9
  98.6 33.6 %all-reduce.51.cloned.1.call-done = f32[2,4,64,256]{3,2,1,0:T(8,128)} async-done(((f32[2,4,64,256]{3,2,1,0:T(8,128)}), f32[2,4,64,256]{3,2,1,0:T(8,128)}) %all-reduce.51.cloned.1.call-update) | async-done | bytes 524304 | tf_op jit(solution)/shard_map/psum | solution.py:135
  132.2 1.6 %constant_dynamic-slice_fusion = f32[2,4,16,256]{3,2,1,0:T(8,128)} fusion(f32[2,4,64,256]{3,2,1,0:T(8,128)} %all-reduce.51.cloned.1.call-done, s32[]{:T(128)S(6)} %select_n.43), kind=kLoop, calls=%fused_computation.276 | loop fusion | bytes 262148 | tf_op jit(solution)/shard_map/dynamic_slice | solution.py:137
  (57 shorter events, 8.6 us)
Async XLA Ops:
  7.2 9.7 %copy-start.3 = (bf16[1,2,3,4,64,256]{5,4,3,2,1,0:T(8,128)(2,1)S(1)}, bf16[1,2,3,4,64,256]{5,4,3,2,1,0:T(8,128)(2,1)}, u32[]{:S(2)}) copy-start(bf16[1,2,3,4,64,256]{5,4,3,2,1,0:T(8,128)(2,1)} %param.12) | copy-start | bytes 2359300
  7.2 125.0 %all-reduce.51.cloned.1.call-start = ((), (), s32[]{:S(2)}) async-start(), calls=%async_computation | async-start | bytes 1048576 | tf_op jit(solution)/shard_map/psum | solution.py:135
  9.2 30.1 %collective-permute-start = (f32[1,2,3,1,64,256]{5,4,3,1,2,0:T(8,128)}, f32[1,2,3,1,64,256]{5,4,3,1,2,0:T(8,128)}, u32[]{:S(2)}, u32[]{:S(2)}) collective-permute-start(f32[1,2,3,1,64,256]{5,4,3,1,2,0:T(8,128)} %copy.50), channel_id=1, source_target_pairs={{0,1},{1,2},{2,3},{3,4},{4,5},{5,6},{6,7},{8,9},{9,10},{10,11},{11... | collective-permute-start | bytes 1179656 | tf_op jit(solution)/shard_map/ppermute | solution.py:21
  13.4 12.1 %copy-start.7 = (s32[64]{0:T(128)S(1)}, s32[64]{0:T(128)}, u32[]{:S(2)}) copy-start(s32[64]{0:T(128)} %param.15) | copy-start | bytes 772
  13.4 12.1 %copy-start = (bf16[1,2,3,4,64,256]{5,4,3,2,1,0:T(8,128)(2,1)S(1)}, bf16[1,2,3,4,64,256]{5,4,3,2,1,0:T(8,128)(2,1)}, u32[]{:S(2)}) copy-start(bf16[1,2,3,4,64,256]{5,4,3,2,1,0:T(8,128)(2,1)} %param.11) | copy-start | bytes 2359300
  13.4 27.1 %collective-permute-start.1 = (f32[1,2,3,1,64,256]{5,4,3,1,2,0:T(8,128)}, f32[1,2,3,1,64,256]{5,4,3,1,2,0:T(8,128)}, u32[]{:S(2)}, u32[]{:S(2)}) collective-permute-start(f32[1,2,3,1,64,256]{5,4,3,1,2,0:T(8,128)} %copy.51), channel_id=1, source_target_pairs={{1,0},{2,1},{3,2},{4,3},{5,4},{6,5},{7,6},{9,8},{10,9},{11,10},{12... | collective-permute-start | bytes 1179656 | tf_op jit(solution)/shard_map/ppermute | solution.py:23
  18.0 33.6 %collective-permute-start.4 = (f32[1,2,3,1,64,256]{5,4,3,1,2,0:T(8,128)}, f32[1,2,3,1,64,256]{5,4,3,1,2,0:T(8,128)}, u32[]{:S(2)}, u32[]{:S(2)}) collective-permute-start(f32[1,2,3,1,64,256]{5,4,3,1,2,0:T(8,128)} %get-tuple-element.30), channel_id=1, source_target_pairs={{0,1},{1,2},{2,3},{3,4},{4,5},{5,6},{6,7},{8,9},{9,10},{10,11},{11... | collective-permute-start | bytes 1179656 | tf_op jit(solution)/shard_map/ppermute | solution.py:21
  20.5 31.1 %collective-permute-start.5 = (f32[1,2,3,1,64,256]{5,4,3,1,2,0:T(8,128)}, f32[1,2,3,1,64,256]{5,4,3,1,2,0:T(8,128)}, u32[]{:S(2)}, u32[]{:S(2)}) collective-permute-start(f32[1,2,3,1,64,256]{5,4,3,1,2,0:T(8,128)} %get-tuple-element.31), channel_id=1, source_target_pairs={{1,0},{2,1},{3,2},{4,3},{5,4},{6,5},{7,6},{9,8},{10,9},{11,10},{12... | collective-permute-start | bytes 1179656 | tf_op jit(solution)/shard_map/ppermute | solution.py:23
  42.3 1.0 copy-start.1
  42.3 1.0 copy-start.2
  42.3 1.6 %copy-start.4 = (f32[1,2,3,4,64,256]{5,4,3,2,1,0:T(8,128)S(1)}, f32[1,2,3,4,64,256]{5,4,3,2,1,0:T(8,128)}, u32[]{:S(2)}) copy-start(f32[1,2,3,4,64,256]{5,4,3,2,1,0:T(8,128)} %convert_element_type.71) | copy-start | bytes 4718596
  44.9 19.2 %collective-permute-start.2 = (f32[1,2,3,1,64,256]{5,4,3,1,2,0:T(8,128)S(1)}, f32[1,2,3,1,64,256]{5,4,3,1,2,0:T(8,128)S(1)}, u32[]{:S(2)}, u32[]{:S(2)}) collective-permute-start(f32[1,2,3,1,64,256]{5,4,3,1,2,0:T(8,128)S(1)} %copy.52), channel_id=1, source_target_pairs={{0,1},{1,2},{2,3},{3,4},{4,5},{5,6},{6,7},{8,9},{9,10},{10,11},{11... | collective-permute-start | bytes 1179656 | tf_op jit(solution)/shard_map/ppermute | solution.py:21
  49.3 17.4 %collective-permute-start.3 = (f32[1,2,3,1,64,256]{5,4,3,1,2,0:T(8,128)S(1)}, f32[1,2,3,1,64,256]{5,4,3,1,2,0:T(8,128)S(1)}, u32[]{:S(2)}, u32[]{:S(2)}) collective-permute-start(f32[1,2,3,1,64,256]{5,4,3,1,2,0:T(8,128)S(1)} %copy.53), channel_id=1, source_target_pairs={{1,0},{2,1},{3,2},{4,3},{5,4},{6,5},{7,6},{9,8},{10,9},{11,10},{12... | collective-permute-start | bytes 1179656 | tf_op jit(solution)/shard_map/ppermute | solution.py:23
  70.0 1.1 copy-start.6
  72.5 19.2 %collective-permute-start.6 = (f32[1,2,3,1,64,256]{5,4,3,1,2,0:T(8,128)S(1)}, f32[1,2,3,1,64,256]{5,4,3,1,2,0:T(8,128)S(1)}, u32[]{:S(2)}, u32[]{:S(2)}) collective-permute-start(f32[1,2,3,1,64,256]{5,4,3,1,2,0:T(8,128)S(1)} %get-tuple-element.29), channel_id=1, source_target_pairs={{0,1},{1,2},{2,3},{3,4},{4,5},{5,6},{6,7},{8,9},{9,10},{10,11},{11... | collective-permute-start | bytes 1179656 | tf_op jit(solution)/shard_map/ppermute | solution.py:21
  75.0 22.4 %copy-start.5 = (f32[1,2,3,4,64,256]{5,4,3,2,1,0:T(8,128)}, f32[1,2,3,4,64,256]{5,4,3,2,1,0:T(8,128)S(1)}, u32[]{:S(2)}) copy-start(f32[1,2,3,4,64,256]{5,4,3,2,1,0:T(8,128)S(1)} %fusion.1) | copy-start | bytes 4718596
  75.0 19.7 %collective-permute-start.7 = (f32[1,2,3,1,64,256]{5,4,3,1,2,0:T(8,128)S(1)}, f32[1,2,3,1,64,256]{5,4,3,1,2,0:T(8,128)S(1)}, u32[]{:S(2)}, u32[]{:S(2)}) collective-permute-start(f32[1,2,3,1,64,256]{5,4,3,1,2,0:T(8,128)S(1)} %get-tuple-element.28), channel_id=1, source_target_pairs={{1,0},{2,1},{3,2},{4,3},{5,4},{6,5},{7,6},{9,8},{10,9},{11,10},{12... | collective-permute-start | bytes 1179656 | tf_op jit(solution)/shard_map/ppermute | solution.py:23
Sparse Core Ops, SparseCore 0:
  98.7 33.4 all-reduce.50
where the time goes:
time: 143 us; the launch traced here: 141 us
  waiting for transfers between devices  68 us (48%)
  starting transfers between devices  27.3 us (19%)
  other arithmetic  19.2 us (13%)
  between operations  15.8 us (11%)
  local copies, waits for them, and re-layouts  10.2 us (7%)
    psum x1, waiting for transfers between devices, on_device(): summed = lax.psum(local_grad, 'freq')  33.6 us
    ppermute x4, waiting for transfers between devices, padded_2(): lax.ppermute(tail, axis, [(i, (i + 1) % count) for i in range(ends)])  29.3 us
    ppermute x4, starting transfers between devices, padded_2(): lax.ppermute(head, axis, [((i + 1) % count, i) for i in range(ends)])  14.9 us
    ppermute x4, starting transfers between devices, padded_2(): lax.ppermute(tail, axis, [(i, (i + 1) % count) for i in range(ends)])  12.3 us
    ppermute x4, waiting for transfers between devices, padded_2(): lax.ppermute(head, axis, [((i + 1) % count, i) for i in range(ends)])  5.13 us
    unnamed x23, local copies, waits for them, and re-layouts  4.64 us
    scatter-add x1, other arithmetic, make_source(): counts.at[jnp.clip(cell_x, 0, slab_width - 1), cell_y, cell_z].add(weights)  4.58 us
  transfers between devices with their start and end apart: 9, of which 6 were waited for; matrix products, arithmetic and copies ran while one was open for 11% of the time, Pallas kernels for 0%

commit v1 on v0

v1 whole, which is shorter than its diff:
```python
import functools

import jax
import jax.numpy as jnp
from jax import lax
from jax.experimental import pallas as pl
from jax.experimental.pallas import tpu as pltpu
from jax.sharding import PartitionSpec as P

THETA = 0.5
SOURCE_GAIN = 8.0
MESH = pl.DeviceIdType.MESH
E0, E1, A0, A1 = 0, 1, 2, 3


def sweeps_kernel(
    freqs, slabs, tx_max,
    sig_h, sig_v, wave, field_start, adjoint_start, observed, tx_count, tx_cells,
    grad_out, field,
    xs, yz, gs, coef, onehot_row, onehot_z, counts, grad_send, grad_recv,
    halo_send, halo_recv, peer_send, peer_recv,
):
    width, rows, cols = sig_h.shape
    share = rows // freqs
    last = width - 1
    me_f = lax.axis_index("freq")
    me_x = lax.axis_index("gx")
    has_left = me_x > 0
    has_right = me_x < slabs - 1
    scale = wave[0]
    row_id = lax.broadcasted_iota(jnp.int32, (rows, cols), 0)
    col_id = lax.broadcasted_iota(jnp.int32, (rows, cols), 1)

    def up_y(v):
        return jnp.where(row_id == rows - 1, 0.0, pltpu.roll(v, rows - 1, 0))

    def up_z(v):
        return jnp.where(col_id == cols - 1, 0.0, pltpu.roll(v, cols - 1, 1))

    def down_y(v):
        return jnp.where(row_id == 0, 0.0, pltpu.roll(v, 1, 0))

    def down_z(v):
        return jnp.where(col_id == 0, 0.0, pltpu.roll(v, 1, 1))

    def put(s, i, r, vx, vy, vz):
        xs[s, i, r] = vx
        yz[s, i, 0, r] = vy
        yz[s, i, 1, r] = vz
        gs[s, i + 1, 0, r] = vy + (up_y(vx) - vx)
        gs[s, i + 1, 1, r] = vz + (up_z(vx) - vx)

    def fill(s, i, start):
        for r in range(2):
            put(s, i, r, *(start[0, r, c, i].astype(jnp.float32) for c in range(3)))

    def ends(s):
        @pl.when(jnp.logical_not(has_left))
        def _():
            gs[s, 0] = yz[s, 0]

        @pl.when(jnp.logical_not(has_right))
        def _():
            yz[s, width] = jnp.zeros((2, 2, rows, cols), jnp.float32)

    def curl(s, i, r):
        vx, vy, vz = xs[s, i, r], yz[s, i, 0, r], yz[s, i, 1, r]
        hx = (up_y(vz) - vz) - (up_z(vy) - vy)
        hy = gs[s, i + 1, 1, r] - yz[s, i + 1, 1, r]
        hz = yz[s, i + 1, 0, r] - gs[s, i + 1, 0, r]
        hy_before = gs[s, i, 1, r] - vz
        hz_before = vy - gs[s, i, 0, r]
        kx = (hz - down_y(hz)) - (hy - down_z(hy))
        ky = (hx - down_z(hx)) - (hz - hz_before)
        kz = (hy - hy_before) - (hx - down_y(hx))
        return (vx, vy, vz), (kx, ky, kz)

    def update(s, i, rhs):
        real, k_real = curl(s, i, 0)
        imag, k_imag = curl(s, i, 1)
        out_re, out_im = [], []
        for c in range(3):
            which = 1 if c == 2 else 0
            coupling = scale * (sig_v if which else sig_h)[i]
            main, cross = coef[which, 0, i], coef[which, 1, i]
            b_re, b_im = rhs(c, i)
            r_re = b_re - (k_real[c] - coupling * imag[c])
            r_im = b_im - (k_imag[c] + coupling * real[c])
            out_re.append(real[c] + (main * r_re + cross * r_im))
            out_im.append(imag[c] + (main * r_im - cross * r_re))
        return out_re, out_im

    def source(c, i):
        return 0.0, (SOURCE_GAIN * scale) * counts[i] if c == 0 else 0.0

    def misfit(c, i):
        return (
            field[0, 0, c, i] - observed[0, 0, c, i].astype(jnp.float32),
            observed[0, 1, c, i].astype(jnp.float32) - field[0, 1, c, i],
        )

    def advance(s, i, rhs):
        out_re, out_im = update(s, i, rhs)
        put(s + 1, i, 0, *out_re)
        put(s + 1, i, 1, *out_im)

    def finish_field(i):
        out_re, out_im = update(E1, i, source)
        for c in range(3):
            field[0, 0, c, i] = out_re[c]
            field[0, 1, c, i] = out_im[c]

    def finish_grad(i, phase, slot):
        out_re, out_im = update(A1, i, misfit)
        terms = [
            scale * (out_re[c] * field[0, 1, c, i] + out_im[c] * field[0, 0, c, i])
            for c in range(3)
        ]
        for which, term in enumerate((terms[0] + terms[1], terms[2])):
            for f in range(freqs):
                grad_send[phase, f, which, slot] = term[f * share:(f + 1) * share]

    def rightward(s):
        return pltpu.make_async_remote_copy(
            gs.at[s, width], gs.at[s, 0], halo_send.at[s, 0], halo_recv.at[s, 0],
            device_id={"gx": me_x + 1}, device_id_type=MESH,
        )

    def leftward(s):
        return pltpu.make_async_remote_copy(
            yz.at[s, 0], yz.at[s, width], halo_send.at[s, 1], halo_recv.at[s, 1],
            device_id={"gx": me_x - 1}, device_id_type=MESH,
        )

    def send_right(s):
        pl.when(has_right)(lambda: rightward(s).start())

    def send_left(s):
        pl.when(has_left)(lambda: leftward(s).start())

    def wait_left(s):
        pl.when(has_left)(lambda: rightward(s).wait_recv())

    def wait_right(s):
        pl.when(has_right)(lambda: leftward(s).wait_recv())

    def to_peer(phase, off):
        peer = lax.rem(me_f + off, freqs)
        return pltpu.make_async_remote_copy(
            grad_send.at[phase, peer], grad_recv.at[phase, off],
            peer_send.at[phase, off], peer_recv.at[phase, off],
            device_id={"freq": peer}, device_id_type=MESH,
        )

    def inner(body):
        if width > 2:
            lax.fori_loop(1, last, lambda i, _: (body(i), 0)[1], 0)

    barrier = pltpu.get_barrier_semaphore()

    @pl.when(has_left)
    def _():
        pl.semaphore_signal(barrier, 1, device_id={"gx": me_x - 1}, device_id_type=MESH)

    @pl.when(has_right)
    def _():
        pl.semaphore_signal(barrier, 1, device_id={"gx": me_x + 1}, device_id_type=MESH)

    for off in range(1, freqs):
        pl.semaphore_signal(
            barrier, 1, device_id={"freq": lax.rem(me_f + off, freqs)}, device_id_type=MESH
        )
    fill(E0, 0, field_start)
    fill(E0, last, field_start)
    pl.semaphore_wait(
        barrier, freqs - 1 + has_left.astype(jnp.int32) + has_right.astype(jnp.int32)
    )
    send_left(E0)
    send_right(E0)
    ends(E0)
    fill(A0, 0, adjoint_start)
    fill(A0, last, adjoint_start)
    ends(A0)

    def prepare(i):
        for which, sig in enumerate((sig_h, sig_v)):
            coupling = scale * sig[i]
            part = THETA / (16.0 + coupling * coupling)
            coef[which, 0, i] = 4.0 * part
            coef[which, 1, i] = coupling * part

    lax.fori_loop(0, width, lambda i, _: (prepare(i), 0)[1], 0)

    row_line = lax.broadcasted_iota(jnp.int32, (1, width * rows), 1)
    col_line = lax.broadcasted_iota(jnp.int32, (1, cols), 1)

    def mark(t, _):
        cell = tx_cells[t]
        row = cell // cols
        col = cell - row * cols
        row = jnp.where(t < tx_count[0], row - me_x * (width * rows), -1)
        onehot_row[pl.ds(t, 1), :] = jnp.where(row_line == row, 1.0, 0.0)
        onehot_z[pl.ds(t, 1), :] = jnp.where(col_line == col, 1.0, 0.0)
        return 0

    lax.fori_loop(0, tx_max, mark, 0)
    counts[...] = lax.dot_general(
        onehot_row[...].astype(jnp.bfloat16), onehot_z[...].astype(jnp.bfloat16),
        (((0,), (0,)), ((), ())), preferred_element_type=jnp.float32,
    ).reshape(width, rows, cols)

    inner(lambda i: fill(E0, i, field_start))
    inner(lambda i: fill(A0, i, adjoint_start))
    inner(lambda i: advance(E0, i, source))

    wait_left(E0)
    send_left(A0)
    advance(E0, 0, source)
    send_left(E1)
    wait_right(E0)
    send_right(A0)
    advance(E0, last, source)
    send_right(E1)
    ends(E1)
    inner(finish_field)
    inner(lambda i: advance(A0, i, misfit))

    wait_left(E1)
    finish_field(0)
    wait_left(A0)
    advance(A0, 0, misfit)
    send_left(A1)
    wait_right(E1)
    finish_field(last)
    wait_right(A0)
    advance(A0, last, misfit)
    send_right(A1)
    ends(A1)

    if width > 2:
        lax.fori_loop(1, last, lambda i, _: (finish_grad(i, 0, i - 1), 0)[1], 0)
    for off in range(1, freqs):
        to_peer(0, off).start()
    wait_left(A1)
    finish_grad(0, 1, 0)
    wait_right(A1)
    finish_grad(last, 1, 1)
    for off in range(1, freqs):
        to_peer(1, off).start()

    for phase, layers in ((0, tuple(range(1, last))), (1, (0, last))):
        total = grad_send[phase, me_f]
        for off in range(1, freqs):
            to_peer(phase, off).wait_recv()
            total = total + grad_recv[phase, off]
        for slot, layer in enumerate(layers):
            grad_out[:, layer] = total[:, slot]
    for off in range(1, freqs):
        to_peer(0, off).wait_send()
        to_peer(1, off).wait_send()
    for s in (E0, E1, A0, A1):
        pl.when(has_right)(lambda: rightward(s).wait_send())
        pl.when(has_left)(lambda: leftward(s).wait_send())


def on_device(freqs, slabs, sigma_h, sigma_v, wave_scale, field_start, adjoint_start, observed, tx_count, tx_cells):
    width, rows, cols = sigma_h.shape
    tx_max = tx_cells.shape[0]
    share = rows // freqs
    inner_count = max(width - 2, 2)
    vmem = pl.BlockSpec(memory_space=pltpu.VMEM)
    smem = pl.BlockSpec(memory_space=pltpu.SMEM)
    f32 = jnp.float32
    return pl.pallas_call(
        functools.partial(sweeps_kernel, freqs, slabs, tx_max),
        out_shape=(
            jax.ShapeDtypeStruct((2, width, share, cols), f32),
            jax.ShapeDtypeStruct(field_start.shape, f32),
        ),
        in_specs=[vmem, vmem, smem, vmem, vmem, vmem, smem, smem],
        out_specs=(vmem, vmem),
        scratch_shapes=[
            pltpu.VMEM((4, width, 2, rows, cols), f32),
            pltpu.VMEM((4, width + 1, 2, 2, rows, cols), f32),
            pltpu.VMEM((4, width + 1, 2, 2, rows, cols), f32),
            pltpu.VMEM((2, 2, width, rows, cols), f32),
            pltpu.VMEM((tx_max, width * rows), f32),
            pltpu.VMEM((tx_max, cols), f32),
            pltpu.VMEM((width, rows, cols), f32),
            pltpu.VMEM((2, freqs, 2, inner_count, share, cols), f32),
            pltpu.VMEM((2, freqs, 2, inner_count, share, cols), f32),
            pltpu.SemaphoreType.DMA((4, 2)),
            pltpu.SemaphoreType.DMA((4, 2)),
            pltpu.SemaphoreType.DMA((2, freqs)),
            pltpu.SemaphoreType.DMA((2, freqs)),
        ],
        compiler_params=pltpu.CompilerParams(
            collective_id=0, has_side_effects=True, vmem_limit_bytes=48 * 1024 * 1024
        ),
    )(sigma_h, sigma_v, wave_scale, field_start, adjoint_start, observed, tx_count, tx_cells)


def solution(mesh):
    placed = (
        P("gx", None, None),
        P("gx", None, None),
        P("freq"),
        P("freq", None, None, "gx", None, None),
        P("freq", None, None, "gx", None, None),
        P("freq", None, None, "gx", None, None),
        P(),
        P(),
    )
    return jax.shard_map(
        functools.partial(on_device, mesh.shape["freq"], mesh.shape["gx"]),
        mesh=mesh,
        in_specs=placed,
        out_specs=(P(None, "gx", "freq", None), P("freq", None, None, "gx", None, None)),
        check_vma=False,
    )
```

time: 143 us -> 78.1 us (0.55)
  the two profiles are of different devices: /device:TPU:8 before, /device:TPU:15 now
where the time goes in v1:
time: 78.1 us; the launch traced here: 77.8 us
  Pallas kernels  68.1 us (87%)
  local copies, waits for them, and re-layouts  7.75 us (10%)
  between operations  1.95 us (2%)
    pallas_call x1, Pallas kernels, on_device(): pl.pallas_call(functools.partial(sweeps_kernel, freqs, slabs, tx_max), ou...  68.1 us
    unnamed x14, local copies, waits for them, and re-layouts  7.75 us

profile of v1, /device:TPU:15, one launch (start us, length us, event | category | flops | bytes accessed | tf_op | source)
XLA Modules:
  0.0 77.8 jit_solution(4076979128383105514)
XLA Ops:
  1.9 0.0 copy-start
  1.9 1.1 %copy-done = bf16[1,2,3,4,64,256]{5,4,3,2,1,0:T(8,128)(2,1)S(1)} copy-done((bf16[1,2,3,4,64,256]{5,4,3,2,1,0:T(8,128)(2,1)S(1)}, bf16[1,2,3,4,64,256]{5,4,3,2,1,0:T(8,128)(2,1)}, u32[]{:S(2)}) %copy-start) | copy-done | bytes 786456
  3.1 0.0 copy-start.1
  3.1 1.1 %copy-done.1 = bf16[1,2,3,4,64,256]{5,4,3,2,1,0:T(8,128)(2,1)S(1)} copy-done((bf16[1,2,3,4,64,256]{5,4,3,2,1,0:T(8,128)(2,1)S(1)}, bf16[1,2,3,4,64,256]{5,4,3,2,1,0:T(8,128)(2,1)}, u32[]{:S(2)}) %copy-start.1) | copy-done | bytes 786456
  4.2 0.0 copy-start.2
  4.2 1.1 %copy-done.2 = bf16[1,2,3,4,64,256]{5,4,3,2,1,0:T(8,128)(2,1)S(1)} copy-done((bf16[1,2,3,4,64,256]{5,4,3,2,1,0:T(8,128)(2,1)S(1)}, bf16[1,2,3,4,64,256]{5,4,3,2,1,0:T(8,128)(2,1)}, u32[]{:S(2)}) %copy-start.2) | copy-done | bytes 786456
  5.3 0.0 copy-start.3
  5.3 0.9 %copy-done.3 = f32[4,64,256]{2,1,0:T(8,128)S(1)} copy-done((f32[4,64,256]{2,1,0:T(8,128)S(1)}, f32[4,64,256]{2,1,0:T(8,128)}, u32[]{:S(2)}) %copy-start.3) | copy-done | bytes 262168
  6.3 0.0 copy-start.4
  6.3 0.9 %copy-done.4 = f32[4,64,256]{2,1,0:T(8,128)S(1)} copy-done((f32[4,64,256]{2,1,0:T(8,128)S(1)}, f32[4,64,256]{2,1,0:T(8,128)}, u32[]{:S(2)}) %copy-start.4) | copy-done | bytes 262168
  7.2 0.0 copy-start.5
  7.2 0.7 copy-done.5
  7.9 68.1 %shard_map.95 = (f32[2,4,16,256]{3,2,1,0:T(8,128)S(1)}, f32[1,2,3,4,64,256]{5,4,3,2,1,0:T(8,128)S(1)}) custom-call(f32[4,64,256]{2,1,0:T(8,128)S(1)} %copy-done.3, f32[4,64,256]{2,1,0:T(8,128)S(1)} %copy-done.4, f32[1]{0:T(128)S(6)} %copy.12.wave, bf16[1,2,3,4,64,256]{5,4,3,2,1,0:T(8,128)(2,1)S(1)} %copy-done, bf16[1,2,3,4,64,256]{5,4,3,2,1,0:T(8,128)(2,1)S(1)} %copy-done.1, ...), custom_call_target="tpu_custom_call" | custom-call | tf_op jit(solution)/shard_map/pallas_call | solution.py:274
  76.0 0.7 copy.14
  76.6 1.1 %copy.15 = f32[1,2,3,4,64,256]{5,4,3,2,1,0:T(8,128)} copy(f32[1,2,3,4,64,256]{5,4,3,2,1,0:T(8,128)S(1)} %get-tuple-element.5) | data formatting | bytes 3145728
Async XLA Ops:
  1.9 1.1 %copy-start = (bf16[1,2,3,4,64,256]{5,4,3,2,1,0:T(8,128)(2,1)S(1)}, bf16[1,2,3,4,64,256]{5,4,3,2,1,0:T(8,128)(2,1)}, u32[]{:S(2)}) copy-start(bf16[1,2,3,4,64,256]{5,4,3,2,1,0:T(8,128)(2,1)} %field_start.1) | copy-start | bytes 2359300
  3.1 1.1 %copy-start.1 = (bf16[1,2,3,4,64,256]{5,4,3,2,1,0:T(8,128)(2,1)S(1)}, bf16[1,2,3,4,64,256]{5,4,3,2,1,0:T(8,128)(2,1)}, u32[]{:S(2)}) copy-start(bf16[1,2,3,4,64,256]{5,4,3,2,1,0:T(8,128)(2,1)} %adjoint_start.1) | copy-start | bytes 2359300
  4.2 1.1 %copy-start.2 = (bf16[1,2,3,4,64,256]{5,4,3,2,1,0:T(8,128)(2,1)S(1)}, bf16[1,2,3,4,64,256]{5,4,3,2,1,0:T(8,128)(2,1)}, u32[]{:S(2)}) copy-start(bf16[1,2,3,4,64,256]{5,4,3,2,1,0:T(8,128)(2,1)} %observed.1) | copy-start | bytes 2359300
  5.3 0.9 %copy-start.3 = (f32[4,64,256]{2,1,0:T(8,128)S(1)}, f32[4,64,256]{2,1,0:T(8,128)}, u32[]{:S(2)}) copy-start(f32[4,64,256]{2,1,0:T(8,128)} %sig_h.1) | copy-start | bytes 786436
  6.3 0.9 %copy-start.4 = (f32[4,64,256]{2,1,0:T(8,128)S(1)}, f32[4,64,256]{2,1,0:T(8,128)}, u32[]{:S(2)}) copy-start(f32[4,64,256]{2,1,0:T(8,128)} %sig_v.1) | copy-start | bytes 786436
  7.2 0.7 copy-start.5

commit v2 on v1

v2 whole, which is shorter than its diff:
```python
import functools

import jax
import jax.numpy as jnp
from jax import lax
from jax.experimental import pallas as pl
from jax.experimental.pallas import tpu as pltpu
from jax.sharding import PartitionSpec as P

THETA = 0.5
SOURCE_GAIN = 8.0
MESH = pl.DeviceIdType.MESH
E0, E1, A0, A1 = 0, 1, 2, 3


def sweeps_kernel(
    freqs, slabs, tx_max,
    sig_h_in, sig_v_in, wave, field_in, adjoint_in, observed_in, tx_count, tx_cells,
    grad_out, field,
    sig_h, sig_v, field_start, adjoint_start, observed,
    xs, yz, gs, coef, onehot_row, onehot_z, counts, grad_send, grad_recv,
    load_sem, halo_send, halo_recv, peer_send, peer_recv,
):
    width, rows, cols = sig_h.shape
    share = rows // freqs
    last = width - 1
    half = rows // 2
    early = half - 8
    whole = (0, rows)
    cut = {E0: (early, early - 8), E1: (early, early), A0: (early, early), A1: (half, early)}
    me_f = lax.axis_index("freq")
    me_x = lax.axis_index("gx")
    has_left = me_x > 0
    has_right = me_x < slabs - 1
    scale = wave[0]

    def up_y(v, top):
        moved = pltpu.roll(v, v.shape[0] - 1, 0)
        if not top:
            return moved
        row_id = lax.broadcasted_iota(jnp.int32, v.shape, 0)
        return jnp.where(row_id == v.shape[0] - 1, 0.0, moved)

    def down_y(v, bottom):
        moved = pltpu.roll(v, 1, 0)
        if not bottom:
            return moved
        return jnp.where(lax.broadcasted_iota(jnp.int32, v.shape, 0) == 0, 0.0, moved)

    def up_z(v):
        col_id = lax.broadcasted_iota(jnp.int32, v.shape, 1)
        return jnp.where(col_id == cols - 1, 0.0, pltpu.roll(v, cols - 1, 1))

    def down_z(v):
        col_id = lax.broadcasted_iota(jnp.int32, v.shape, 1)
        return jnp.where(col_id == 0, 0.0, pltpu.roll(v, 1, 1))

    def put(s, i, r, part, vx, vy, vz):
        lo, hi = part
        xs[s, i, r, lo:hi] = vx
        yz[s, i, 0, r, lo:hi] = vy
        yz[s, i, 1, r, lo:hi] = vz
        if hi == rows:
            above = up_y(vx, True)
        else:
            above = up_y(xs[s, i, r, lo:hi + 8], False)[:hi - lo]
        gs[s, i + 1, 0, r, lo:hi] = vy + (above - vx)
        gs[s, i + 1, 1, r, lo:hi] = vz + (up_z(vx) - vx)

    def fill(s, i, start):
        for r in range(2):
            put(s, i, r, whole, *(start[r, c, i].astype(jnp.float32) for c in range(3)))

    def left_end(s, part):
        lo, hi = part

        @pl.when(jnp.logical_not(has_left))
        def _():
            gs[s, 0, :, :, lo:hi] = yz[s, 0, :, :, lo:hi]

    def curl(s, i, r, part):
        lo, hi = part
        w0, w1 = max(lo - 8, 0), min(hi + 8, rows)

        def crop(v):
            return v[lo - w0:hi - w0]

        vx = xs[s, i, r, lo:hi]
        wide_y, wide_z = yz[s, i, 0, r, w0:w1], yz[s, i, 1, r, w0:w1]
        hx = (up_y(wide_z, w1 == rows) - wide_z) - (up_z(wide_y) - wide_y)
        hz = yz[s, i + 1, 0, r, w0:w1] - gs[s, i + 1, 0, r, w0:w1]
        hy = gs[s, i + 1, 1, r, lo:hi] - yz[s, i + 1, 1, r, lo:hi]
        vy, vz = crop(wide_y), crop(wide_z)
        hy_before = gs[s, i, 1, r, lo:hi] - vz
        hz_before = vy - gs[s, i, 0, r, lo:hi]
        hx_c, hz_c = crop(hx), crop(hz)
        kx = (hz_c - crop(down_y(hz, w0 == 0))) - (hy - down_z(hy))
        ky = (hx_c - down_z(hx_c)) - (hz_c - hz_before)
        kz = (hy - hy_before) - (hx_c - crop(down_y(hx, w0 == 0)))
        return (vx, vy, vz), (kx, ky, kz)

    def update(s, i, rhs, part):
        lo, hi = part
        real, k_real = curl(s, i, 0, part)
        imag, k_imag = curl(s, i, 1, part)
        out_re, out_im = [], []
        for c in range(3):
            which = 1 if c == 2 else 0
            coupling = scale * (sig_v if which else sig_h)[i, lo:hi]
            main, cross = coef[which, 0, i, lo:hi], coef[which, 1, i, lo:hi]
            b_re, b_im = rhs(c, i, part)
            r_re = b_re - (k_real[c] - coupling * imag[c])
            r_im = b_im - (k_imag[c] + coupling * real[c])
            out_re.append(real[c] + (main * r_re + cross * r_im))
            out_im.append(imag[c] + (main * r_im - cross * r_re))
        return out_re, out_im

    def source(c, i, part):
        lo, hi = part
        return 0.0, (SOURCE_GAIN * scale) * counts[i, lo:hi] if c == 0 else 0.0

    def misfit(c, i, part):
        lo, hi = part
        from_row = lo // 16 * 16
        to_row = (hi + 15) // 16 * 16
        seen = [
            observed[r, c, i, from_row:to_row].astype(jnp.float32)[lo - from_row:hi - from_row]
            for r in range(2)
        ]
        return field[0, 0, c, i, lo:hi] - seen[0], seen[1] - field[0, 1, c, i, lo:hi]

    def advance(s, i, rhs, part=whole):
        out_re, out_im = update(s, i, rhs, part)
        put(s + 1, i, 0, part, *out_re)
        put(s + 1, i, 1, part, *out_im)

    def finish_field(i, part=whole):
        lo, hi = part
        out_re, out_im = update(E1, i, source, part)
        for c in range(3):
            field[0, 0, c, i, lo:hi] = out_re[c]
            field[0, 1, c, i, lo:hi] = out_im[c]

    def finish_grad(i, phase, slot, part=whole):
        lo, hi = part
        out_re, out_im = update(A1, i, misfit, part)
        terms = [
            scale * (out_re[c] * field[0, 1, c, i, lo:hi] + out_im[c] * field[0, 0, c, i, lo:hi])
            for c in range(3)
        ]
        for which, term in enumerate((terms[0] + terms[1], terms[2])):
            for f in range(lo // share, hi // share):
                at = f * share - lo
                grad_send[phase, f, which, slot] = term[at:at + share]

    def piece(s, way, k):
        edge = cut[s][way]
        return pl.ds(edge, rows - edge) if k == 0 else pl.ds(0, edge)

    def rightward(s, k):
        at = piece(s, 0, k)
        return pltpu.make_async_remote_copy(
            gs.at[s, width, :, :, at], gs.at[s, 0, :, :, at],
            halo_send.at[s, 0, k], halo_recv.at[s, 0, k],
            device_id={"gx": me_x + 1}, device_id_type=MESH,
        )

    def leftward(s, k):
        at = piece(s, 1, k)
        return pltpu.make_async_remote_copy(
            yz.at[s, 0, :, :, at], yz.at[s, width, :, :, at],
            halo_send.at[s, 1, k], halo_recv.at[s, 1, k],
            device_id={"gx": me_x - 1}, device_id_type=MESH,
        )

    def send_right(s, k):
        pl.when(has_right)(lambda: rightward(s, k).start())

    def send_left(s, k):
        pl.when(has_left)(lambda: leftward(s, k).start())

    def wait_left(s, k):
        pl.when(has_left)(lambda: rightward(s, k).wait_recv())

    def wait_right(s, k):
        pl.when(has_right)(lambda: leftward(s, k).wait_recv())

    def to_peer(phase, off):
        peer = lax.rem(me_f + off, freqs)
        return pltpu.make_async_remote_copy(
            grad_send.at[phase, peer], grad_recv.at[phase, off],
            peer_send.at[phase, off], peer_recv.at[phase, off],
            device_id={"freq": peer}, device_id_type=MESH,
        )

    def inner(body):
        if width > 2:
            lax.fori_loop(1, last, lambda i, _: (body(i), 0)[1], 0)

    loads = [
        pltpu.make_async_copy(src, dst, load_sem.at[n])
        for n, (src, dst) in enumerate((
            (field_in.at[0, :, :, 0], field_start.at[:, :, 0]),
            (field_in.at[0, :, :, last], field_start.at[:, :, last]),
            (field_in.at[0, :, :, pl.ds(1, last - 1)], field_start.at[:, :, pl.ds(1, last - 1)]),
            (sig_h_in, sig_h),
            (sig_v_in, sig_v),
            (adjoint_in.at[0], adjoint_start),
            (observed_in.at[0], observed),
        ))
    ]
    for load in loads:
        load.start()
    barrier = pltpu.get_barrier_semaphore()

    @pl.when(has_left)
    def _():
        pl.semaphore_signal(barrier, 1, device_id={"gx": me_x - 1}, device_id_type=MESH)

    @pl.when(has_right)
    def _():
        pl.semaphore_signal(barrier, 1, device_id={"gx": me_x + 1}, device_id_type=MESH)

    for off in range(1, freqs):
        pl.semaphore_signal(
            barrier, 1, device_id={"freq": lax.rem(me_f + off, freqs)}, device_id_type=MESH
        )
    loads[0].wait()
    fill(E0, 0, field_start)
    loads[1].wait()
    fill(E0, last, field_start)
    pl.semaphore_wait(
        barrier, freqs - 1 + has_left.astype(jnp.int32) + has_right.astype(jnp.int32)
    )
    for k in range(2):
        send_left(E0, k)
        send_right(E0, k)

    @pl.when(jnp.logical_not(has_right))
    def _():
        for s in (E0, E1, A0, A1):
            yz[s, width] = jnp.zeros((2, 2, rows, cols), jnp.float32)

    left_end(E0, whole)
    for load in loads[2:]:
        load.wait()

    def prepare(i):
        for which, sig in enumerate((sig_h, sig_v)):
            coupling = scale * sig[i]
            part = THETA / (16.0 + coupling * coupling)
            coef[which, 0, i] = 4.0 * part
            coef[which, 1, i] = coupling * part

    lax.fori_loop(0, width, lambda i, _: (prepare(i), 0)[1], 0)

    row_line = lax.broadcasted_iota(jnp.int32, (1, width * rows), 1)
    col_line = lax.broadcasted_iota(jnp.int32, (1, cols), 1)

    def mark(t, _):
        cell = tx_cells[t]
        row = cell // cols
        col = cell - row * cols
        row = jnp.where(t < tx_count[0], row - me_x * (width * rows), -1)
        onehot_row[pl.ds(t, 1), :] = jnp.where(row_line == row, 1.0, 0.0)
        onehot_z[pl.ds(t, 1), :] = jnp.where(col_line == col, 1.0, 0.0)
        return 0

    lax.fori_loop(0, tx_max, mark, 0)
    counts[...] = lax.dot_general(
        onehot_row[...].astype(jnp.bfloat16), onehot_z[...].astype(jnp.bfloat16),
        (((0,), (0,)), ((), ())), preferred_element_type=jnp.float32,
    ).reshape(width, rows, cols)

    inner(lambda i: fill(E0, i, field_start))
    fill(A0, 0, adjoint_start)
    fill(A0, last, adjoint_start)
    left_end(A0, whole)

    for k, part in enumerate(((early, rows), (0, early))):
        wait_left(E0, k)
        if k == 0:
            send_left(A0, 0)
        advance(E0, 0, source, part)
        send_left(E1, k)
        left_end(E1, part)
        wait_right(E0, k)
        if k == 0:
            send_right(A0, 0)
        advance(E0, last, source, part)
        send_right(E1, k)
        if k == 0:
            send_left(A0, 1)
            send_right(A0, 1)
            inner(lambda i: advance(E0, i, source))
            inner(lambda i: fill(A0, i, adjoint_start))

    inner(finish_field)
    inner(lambda i: advance(A0, i, misfit))

    for k, (near, far) in enumerate((((early, rows), (half, rows)), ((0, early), (0, half)))):
        wait_left(E1, k)
        finish_field(0, near)
        wait_left(A0, k)
        advance(A0, 0, misfit, near)
        send_left(A1, k)
        left_end(A1, near)
        wait_right(E1, k)
        finish_field(last, far)
        wait_right(A0, k)
        advance(A0, last, misfit, far)
        send_right(A1, k)

    if width > 2:
        lax.fori_loop(1, last, lambda i, _: (finish_grad(i, 0, i - 1), 0)[1], 0)
    for off in range(1, freqs):
        to_peer(0, off).start()
    for k, part in enumerate(((half, rows), (0, half))):
        wait_left(A1, k)
        finish_grad(0, 1, 0, part)
        wait_right(A1, k)
        finish_grad(last, 1, 1, part)
        for off in range(1, freqs):
            upper = lax.rem(me_f + off, freqs) >= freqs // 2
            pl.when(upper if k == 0 else jnp.logical_not(upper))(
                lambda: to_peer(1, off).start()
            )

    for phase, layers in ((0, tuple(range(1, last))), (1, (0, last))):
        total = grad_send[phase, me_f]
        for off in range(1, freqs):
            to_peer(phase, off).wait_recv()
            total = total + grad_recv[phase, off]
        for slot, layer in enumerate(layers):
            grad_out[:, layer] = total[:, slot]
    for off in range(1, freqs):
        to_peer(0, off).wait_send()
        to_peer(1, off).wait_send()
    for s in (E0, E1, A0, A1):
        for k in range(2):
            pl.when(has_right)(lambda: rightward(s, k).wait_send())
            pl.when(has_left)(lambda: leftward(s, k).wait_send())


def on_device(freqs, slabs, sigma_h, sigma_v, wave_scale, field_start, adjoint_start, observed, tx_count, tx_cells):
    width, rows, cols = sigma_h.shape
    tx_max = tx_cells.shape[0]
    share = rows // freqs
    inner_count = max(width - 2, 2)
    vmem = pl.BlockSpec(memory_space=pltpu.VMEM)
    hbm = pl.BlockSpec(memory_space=pltpu.HBM)
    smem = pl.BlockSpec(memory_space=pltpu.SMEM)
    f32 = jnp.float32
    return pl.pallas_call(
        functools.partial(sweeps_kernel, freqs, slabs, tx_max),
        out_shape=(
            jax.ShapeDtypeStruct((2, width, share, cols), f32),
            jax.ShapeDtypeStruct(field_start.shape, f32),
        ),
        in_specs=[hbm, hbm, smem, hbm, hbm, hbm, smem, smem],
        out_specs=(vmem, vmem),
        scratch_shapes=[
            pltpu.VMEM(sigma_h.shape, f32),
            pltpu.VMEM(sigma_v.shape, f32),
            pltpu.VMEM(field_start.shape[1:], field_start.dtype),
            pltpu.VMEM(adjoint_start.shape[1:], adjoint_start.dtype),
            pltpu.VMEM(observed.shape[1:], observed.dtype),
            pltpu.VMEM((4, width, 2, rows, cols), f32),
            pltpu.VMEM((4, width + 1, 2, 2, rows, cols), f32),
            pltpu.VMEM((4, width + 1, 2, 2, rows, cols), f32),
            pltpu.VMEM((2, 2, width, rows, cols), f32),
            pltpu.VMEM((tx_max, width * rows), f32),
            pltpu.VMEM((tx_max, cols), f32),
            pltpu.VMEM((width, rows, cols), f32),
            pltpu.VMEM((2, freqs, 2, inner_count, share, cols), f32),
            pltpu.VMEM((2, freqs, 2, inner_count, share, cols), f32),
            pltpu.SemaphoreType.DMA((7,)),
            pltpu.SemaphoreType.DMA((4, 2, 2)),
            pltpu.SemaphoreType.DMA((4, 2, 2)),
            pltpu.SemaphoreType.DMA((2, freqs)),
            pltpu.SemaphoreType.DMA((2, freqs)),
        ],
        compiler_params=pltpu.CompilerParams(
            collective_id=0, has_side_effects=True, vmem_limit_bytes=48 * 1024 * 1024
        ),
    )(sigma_h, sigma_v, wave_scale, field_start, adjoint_start, observed, tx_count, tx_cells)


def solution(mesh):
    placed = (
        P("gx", None, None),
        P("gx", None, None),
        P("freq"),
        P("freq", None, None, "gx", None, None),
        P("freq", None, None, "gx", None, None),
        P("freq", None, None, "gx", None, None),
        P(),
        P(),
    )
    return jax.shard_map(
        functools.partial(on_device, mesh.shape["freq"], mesh.shape["gx"]),
        mesh=mesh,
        in_specs=placed,
        out_specs=(P(None, "gx", "freq", None), P("freq", None, None, "gx", None, None)),
        check_vma=False,
    )
```

time: 78.1 us -> 74.5 us (0.954)
  the two profiles are of different devices: /device:TPU:15 before, /device:TPU:8 now
where the time goes in v2:
time: 74.5 us; the launch traced here: 73.4 us
  Pallas kernels  63.8 us (86%)
  local copies, waits for them, and re-layouts  7.75 us (10%)
  between operations  1.95 us (3%)
    pallas_call x1, Pallas kernels, on_device(): pl.pallas_call(functools.partial(sweeps_kernel, freqs, slabs, tx_max), ou...  63.8 us
    unnamed x14, local copies, waits for them, and re-layouts  7.75 us

profile of v2, /device:TPU:8, one launch (start us, length us, event | category | flops | bytes accessed | tf_op | source)
XLA Modules:
  0.0 73.4 jit_solution(4385805566173635005)
XLA Ops:
  1.9 0.0 copy-start
  1.9 1.1 %copy-done = bf16[1,2,3,4,64,256]{5,4,3,2,1,0:T(8,128)(2,1)S(1)} copy-done((bf16[1,2,3,4,64,256]{5,4,3,2,1,0:T(8,128)(2,1)S(1)}, bf16[1,2,3,4,64,256]{5,4,3,2,1,0:T(8,128)(2,1)}, u32[]{:S(2)}) %copy-start) | copy-done | bytes 786456
  3.1 0.0 copy-start.1
  3.1 1.1 %copy-done.1 = bf16[1,2,3,4,64,256]{5,4,3,2,1,0:T(8,128)(2,1)S(1)} copy-done((bf16[1,2,3,4,64,256]{5,4,3,2,1,0:T(8,128)(2,1)S(1)}, bf16[1,2,3,4,64,256]{5,4,3,2,1,0:T(8,128)(2,1)}, u32[]{:S(2)}) %copy-start.1) | copy-done | bytes 786456
  4.2 0.0 copy-start.2
  4.2 1.1 %copy-done.2 = bf16[1,2,3,4,64,256]{5,4,3,2,1,0:T(8,128)(2,1)S(1)} copy-done((bf16[1,2,3,4,64,256]{5,4,3,2,1,0:T(8,128)(2,1)S(1)}, bf16[1,2,3,4,64,256]{5,4,3,2,1,0:T(8,128)(2,1)}, u32[]{:S(2)}) %copy-start.2) | copy-done | bytes 786456
  5.3 0.0 copy-start.3
  5.3 0.9 %copy-done.3 = f32[4,64,256]{2,1,0:T(8,128)S(1)} copy-done((f32[4,64,256]{2,1,0:T(8,128)S(1)}, f32[4,64,256]{2,1,0:T(8,128)}, u32[]{:S(2)}) %copy-start.3) | copy-done | bytes 262168
  6.3 0.0 copy-start.4
  6.3 0.9 %copy-done.4 = f32[4,64,256]{2,1,0:T(8,128)S(1)} copy-done((f32[4,64,256]{2,1,0:T(8,128)S(1)}, f32[4,64,256]{2,1,0:T(8,128)}, u32[]{:S(2)}) %copy-start.4) | copy-done | bytes 262168
  7.2 0.0 copy-start.5
  7.2 0.7 copy-done.5
  7.9 63.8 %shard_map.95 = (f32[2,4,16,256]{3,2,1,0:T(8,128)S(1)}, f32[1,2,3,4,64,256]{5,4,3,2,1,0:T(8,128)S(1)}) custom-call(f32[4,64,256]{2,1,0:T(8,128)S(1)} %copy-done.3, f32[4,64,256]{2,1,0:T(8,128)S(1)} %copy-done.4, f32[1]{0:T(128)S(6)} %copy.12.wave, bf16[1,2,3,4,64,256]{5,4,3,2,1,0:T(8,128)(2,1)S(1)} %copy-done, bf16[1,2,3,4,64,256]{5,4,3,2,1,0:T(8,128)(2,1)S(1)} %copy-done.1, ...), custom_call_target="tpu_custom_call" | custom-call | tf_op jit(solution)/shard_map/pallas_call | solution.py:354
  71.6 0.7 copy.14
  72.3 1.1 %copy.15 = f32[1,2,3,4,64,256]{5,4,3,2,1,0:T(8,128)} copy(f32[1,2,3,4,64,256]{5,4,3,2,1,0:T(8,128)S(1)} %get-tuple-element.5) | data formatting | bytes 3145728
Async XLA Ops:
  1.9 1.1 %copy-start = (bf16[1,2,3,4,64,256]{5,4,3,2,1,0:T(8,128)(2,1)S(1)}, bf16[1,2,3,4,64,256]{5,4,3,2,1,0:T(8,128)(2,1)}, u32[]{:S(2)}) copy-start(bf16[1,2,3,4,64,256]{5,4,3,2,1,0:T(8,128)(2,1)} %field_in.1) | copy-start | bytes 2359300
  3.1 1.1 %copy-start.1 = (bf16[1,2,3,4,64,256]{5,4,3,2,1,0:T(8,128)(2,1)S(1)}, bf16[1,2,3,4,64,256]{5,4,3,2,1,0:T(8,128)(2,1)}, u32[]{:S(2)}) copy-start(bf16[1,2,3,4,64,256]{5,4,3,2,1,0:T(8,128)(2,1)} %adjoint_in.1) | copy-start | bytes 2359300
  4.2 1.1 %copy-start.2 = (bf16[1,2,3,4,64,256]{5,4,3,2,1,0:T(8,128)(2,1)S(1)}, bf16[1,2,3,4,64,256]{5,4,3,2,1,0:T(8,128)(2,1)}, u32[]{:S(2)}) copy-start(bf16[1,2,3,4,64,256]{5,4,3,2,1,0:T(8,128)(2,1)} %observed_in.1) | copy-start | bytes 2359300
  5.3 0.9 %copy-start.3 = (f32[4,64,256]{2,1,0:T(8,128)S(1)}, f32[4,64,256]{2,1,0:T(8,128)}, u32[]{:S(2)}) copy-start(f32[4,64,256]{2,1,0:T(8,128)} %sig_h_in.1) | copy-start | bytes 786436
  6.3 0.9 %copy-start.4 = (f32[4,64,256]{2,1,0:T(8,128)S(1)}, f32[4,64,256]{2,1,0:T(8,128)}, u32[]{:S(2)}) copy-start(f32[4,64,256]{2,1,0:T(8,128)} %sig_v_in.1) | copy-start | bytes 786436
  7.2 0.7 copy-start.5

commit v3 on v2

--- a/solution.py
+++ b/solution.py
@@ -16,10 +16,10 @@
 def sweeps_kernel(
     freqs, slabs, tx_max,
     sig_h_in, sig_v_in, wave, field_in, adjoint_in, observed_in, tx_count, tx_cells,
-    grad_out, field,
-    sig_h, sig_v, field_start, adjoint_start, observed,
+    grad_hbm, field_hbm,
+    grad_out, field, sig_h, sig_v, field_start, adjoint_start, observed,
     xs, yz, gs, coef, onehot_row, onehot_z, counts, grad_send, grad_recv,
-    load_sem, halo_send, halo_recv, peer_send, peer_recv,
+    load_sem, store_sem, halo_send, halo_recv, peer_send, peer_recv,
 ):
     width, rows, cols = sig_h.shape
     share = rows // freqs
@@ -27,7 +27,13 @@
     half = rows // 2
     early = half - 8
     whole = (0, rows)
-    cut = {E0: (early, early - 8), E1: (early, early), A0: (early, early), A1: (half, early)}
+    low = half // 2
+    cut = {
+        E0: ((early, 0), (early - 8, 0)),
+        E1: ((early, 0), (early, 0)),
+        A0: ((early, 0), (early, 0)),
+        A1: ((half, low, 0), (early, low - 8, 0)),
+    }
     me_f = lax.axis_index("freq")
     me_x = lax.axis_index("gx")
     has_left = me_x > 0
@@ -127,7 +133,7 @@
             observed[r, c, i, from_row:to_row].astype(jnp.float32)[lo - from_row:hi - from_row]
             for r in range(2)
         ]
-        return field[0, 0, c, i, lo:hi] - seen[0], seen[1] - field[0, 1, c, i, lo:hi]
+        return field[0, c, i, lo:hi] - seen[0], seen[1] - field[1, c, i, lo:hi]
 
     def advance(s, i, rhs, part=whole):
         out_re, out_im = update(s, i, rhs, part)
@@ -138,14 +144,14 @@
         lo, hi = part
         out_re, out_im = update(E1, i, source, part)
         for c in range(3):
-            field[0, 0, c, i, lo:hi] = out_re[c]
-            field[0, 1, c, i, lo:hi] = out_im[c]
+            field[0, c, i, lo:hi] = out_re[c]
+            field[1, c, i, lo:hi] = out_im[c]
 
     def finish_grad(i, phase, slot, part=whole):
         lo, hi = part
         out_re, out_im = update(A1, i, misfit, part)
         terms = [
-            scale * (out_re[c] * field[0, 1, c, i, lo:hi] + out_im[c] * field[0, 0, c, i, lo:hi])
+            scale * (out_re[c] * field[1, c, i, lo:hi] + out_im[c] * field[0, c, i, lo:hi])
             for c in range(3)
         ]
         for which, term in enumerate((terms[0] + terms[1], terms[2])):
@@ -154,8 +160,8 @@
                 grad_send[phase, f, which, slot] = term[at:at + share]
 
     def piece(s, way, k):
-        edge = cut[s][way]
-        return pl.ds(edge, rows - edge) if k == 0 else pl.ds(0, edge)
+        edges = (rows,) + cut[s][way]
+        return pl.ds(edges[k + 1], edges[k] - edges[k + 1])
 
     def rightward(s, k):
         at = piece(s, 0, k)
@@ -303,26 +309,30 @@
         finish_field(0, near)
         wait_left(A0, k)
         advance(A0, 0, misfit, near)
-        send_left(A1, k)
+        for n in ((0,), (1, 2))[k]:
+            send_left(A1, n)
         left_end(A1, near)
         wait_right(E1, k)
         finish_field(last, far)
         wait_right(A0, k)
         advance(A0, last, misfit, far)
-        send_right(A1, k)
-
+        for n in ((0,), (1, 2))[k]:
+            send_right(A1, n)
+
+    store_field = pltpu.make_async_copy(field, field_hbm.at[0], store_sem.at[0])
+    store_field.start()
     if width > 2:
         lax.fori_loop(1, last, lambda i, _: (finish_grad(i, 0, i - 1), 0)[1], 0)
     for off in range(1, freqs):
         to_peer(0, off).start()
-    for k, part in enumerate(((half, rows), (0, half))):
+    for k, part in enumerate(((half, rows), (low, half), (0, low))):
         wait_left(A1, k)
         finish_grad(0, 1, 0, part)
         wait_right(A1, k)
         finish_grad(last, 1, 1, part)
         for off in range(1, freqs):
-            upper = lax.rem(me_f + off, freqs) >= freqs // 2
-            pl.when(upper if k == 0 else jnp.logical_not(upper))(
+            row = lax.rem(me_f + off, freqs) * share
+            pl.when(jnp.logical_and(row >= part[0], row < part[1]))(
                 lambda: to_peer(1, off).start()
             )
 
@@ -333,13 +343,17 @@
             total = total + grad_recv[phase, off]
         for slot, layer in enumerate(layers):
             grad_out[:, layer] = total[:, slot]
+    store_grad = pltpu.make_async_copy(grad_out, grad_hbm, store_sem.at[1])
+    store_grad.start()
     for off in range(1, freqs):
         to_peer(0, off).wait_send()
         to_peer(1, off).wait_send()
     for s in (E0, E1, A0, A1):
-        for k in range(2):
+        for k in range(len(cut[s][0])):
             pl.when(has_right)(lambda: rightward(s, k).wait_send())
             pl.when(has_left)(lambda: leftward(s, k).wait_send())
+    store_field.wait()
+    store_grad.wait()
 
 
 def on_device(freqs, slabs, sigma_h, sigma_v, wave_scale, field_start, adjoint_start, observed, tx_count, tx_cells):
@@ -347,7 +361,6 @@
     tx_max = tx_cells.shape[0]
     share = rows // freqs
     inner_count = max(width - 2, 2)
-    vmem = pl.BlockSpec(memory_space=pltpu.VMEM)
     hbm = pl.BlockSpec(memory_space=pltpu.HBM)
     smem = pl.BlockSpec(memory_space=pltpu.SMEM)
     f32 = jnp.float32
@@ -358,8 +371,10 @@
             jax.ShapeDtypeStruct(field_start.shape, f32),
         ),
         in_specs=[hbm, hbm, smem, hbm, hbm, hbm, smem, smem],
-        out_specs=(vmem, vmem),
+        out_specs=(hbm, hbm),
         scratch_shapes=[
+            pltpu.VMEM((2, width, share, cols), f32),
+            pltpu.VMEM(field_start.shape[1:], f32),
             pltpu.VMEM(sigma_h.shape, f32),
             pltpu.VMEM(sigma_v.shape, f32),
             pltpu.VMEM(field_start.shape[1:], field_start.dtype),
@@ -375,13 +390,14 @@
             pltpu.VMEM((2, freqs, 2, inner_count, share, cols), f32),
             pltpu.VMEM((2, freqs, 2, inner_count, share, cols), f32),
             pltpu.SemaphoreType.DMA((7,)),
-            pltpu.SemaphoreType.DMA((4, 2, 2)),
-            pltpu.SemaphoreType.DMA((4, 2, 2)),
+            pltpu.SemaphoreType.DMA((2,)),
+            pltpu.SemaphoreType.DMA((4, 2, 3)),
+            pltpu.SemaphoreType.DMA((4, 2, 3)),
             pltpu.SemaphoreType.DMA((2, freqs)),
             pltpu.SemaphoreType.DMA((2, freqs)),
         ],
         compiler_params=pltpu.CompilerParams(
-            collective_id=0, has_side_effects=True, vmem_limit_bytes=48 * 1024 * 1024
+            collective_id=0, has_side_effects=True, vmem_limit_bytes=(64 * 1024 - 64) * 1024
         ),
     )(sigma_h, sigma_v, wave_scale, field_start, adjoint_start, observed, tx_count, tx_cells)
 

time: 74.5 us -> 70.8 us (0.950); the launches traced: 73.4 us -> 70.6 us
  local copies, waits for them, and re-layouts: 7.75 us -> 4.27 us
    unnamed x14 -> x2, local copies, waits for them, and re-layouts: 7.75 us -> 4.27 us
where the time goes in v3:
time: 70.8 us; the launch traced here: 70.6 us
  Pallas kernels  64.4 us (91%)
  local copies, waits for them, and re-layouts  4.27 us (6%)
  between operations  1.93 us (3%)
    pallas_call x1, Pallas kernels, on_device(): pl.pallas_call(functools.partial(sweeps_kernel, freqs, slabs, tx_max), ou...  64.4 us
    unnamed x2, local copies, waits for them, and re-layouts  4.27 us

profile of v3, /device:TPU:8, one launch (start us, length us, event | category | flops | bytes accessed | tf_op | source)
XLA Modules:
  0.0 70.6 jit_solution(14107350074657001796)
XLA Ops:
  1.9 64.4 %shard_map.95 = (f32[2,4,16,256]{3,2,1,0:T(8,128)}, f32[1,2,3,4,64,256]{5,4,3,2,1,0:T(8,128)}) custom-call(f32[4,64,256]{2,1,0:T(8,128)} %sig_h_in.1, f32[4,64,256]{2,1,0:T(8,128)} %sig_v_in.1, f32[1]{0:T(128)S(6)} %copy.12.wave, bf16[1,2,3,4,64,256]{5,4,3,2,1,0:T(8,128)(2,1)} %field_in.1, bf16[1,2,3,4,64,256]{5,4,3,2,1,0:T(8,128)(2,1)} %adjoint_in.1, ...), custom_call_target="tpu_custom_call" | custom-call | tf_op jit(solution)/shard_map/pallas_call | solution.py:367
  66.3 1.6 %copy.14 = f32[2,4,16,256]{3,2,1,0:T(8,128)} copy(f32[2,4,16,256]{3,2,1,0:T(8,128)} %get-tuple-element.4) | data formatting | bytes 262144
  67.9 2.7 %copy.15 = f32[1,2,3,4,64,256]{5,4,3,2,1,0:T(8,128)} copy(f32[1,2,3,4,64,256]{5,4,3,2,1,0:T(8,128)} %get-tuple-element.5) | data formatting | bytes 3145728

commit v4 on v3

--- a/solution.py
+++ b/solution.py
@@ -250,6 +250,12 @@
     left_end(E0, whole)
     for load in loads[2:]:
         load.wait()
+    fill(A0, 0, adjoint_start)
+    fill(A0, last, adjoint_start)
+    for k in range(2):
+        send_left(A0, k)
+        send_right(A0, k)
+    left_end(A0, whole)
 
     def prepare(i):
         for which, sig in enumerate((sig_h, sig_v)):
@@ -279,27 +285,17 @@
     ).reshape(width, rows, cols)
 
     inner(lambda i: fill(E0, i, field_start))
-    fill(A0, 0, adjoint_start)
-    fill(A0, last, adjoint_start)
-    left_end(A0, whole)
+    inner(lambda i: fill(A0, i, adjoint_start))
+    inner(lambda i: advance(E0, i, source))
 
     for k, part in enumerate(((early, rows), (0, early))):
         wait_left(E0, k)
-        if k == 0:
-            send_left(A0, 0)
         advance(E0, 0, source, part)
         send_left(E1, k)
         left_end(E1, part)
         wait_right(E0, k)
-        if k == 0:
-            send_right(A0, 0)
         advance(E0, last, source, part)
         send_right(E1, k)
-        if k == 0:
-            send_left(A0, 1)
-            send_right(A0, 1)
-            inner(lambda i: advance(E0, i, source))
-            inner(lambda i: fill(A0, i, adjoint_start))
 
     inner(finish_field)
     inner(lambda i: advance(A0, i, misfit))
@@ -356,6 +352,20 @@
     store_grad.wait()
 
 
+def hand_over_kernel(grad_in, field_in, grad_out, field_out, grad, field, sems):
+    places = [(field_in.at[0, r, c], field.at[r, c], field_out.at[0, r, c]) for r in range(2) for c in range(3)]
+    places += [(grad_in.at[n], grad.at[n], grad_out.at[n]) for n in range(2)]
+    reads = [pltpu.make_async_copy(a, b, sems.at[0, n]) for n, (a, b, _) in enumerate(places)]
+    writes = [pltpu.make_async_copy(b, c, sems.at[1, n]) for n, (_, b, c) in enumerate(places)]
+    for read in reads:
+        read.start()
+    for read, write in zip(reads, writes):
+        read.wait()
+        write.start()
+    for write in writes:
+        write.wait()
+
+
 def on_device(freqs, slabs, sigma_h, sigma_v, wave_scale, field_start, adjoint_start, observed, tx_count, tx_cells):
     width, rows, cols = sigma_h.shape
     tx_max = tx_cells.shape[0]
@@ -364,7 +374,7 @@
     hbm = pl.BlockSpec(memory_space=pltpu.HBM)
     smem = pl.BlockSpec(memory_space=pltpu.SMEM)
     f32 = jnp.float32
-    return pl.pallas_call(
+    grad, field = pl.pallas_call(
         functools.partial(sweeps_kernel, freqs, slabs, tx_max),
         out_shape=(
             jax.ShapeDtypeStruct((2, width, share, cols), f32),
@@ -400,6 +410,18 @@
             collective_id=0, has_side_effects=True, vmem_limit_bytes=(64 * 1024 - 64) * 1024
         ),
     )(sigma_h, sigma_v, wave_scale, field_start, adjoint_start, observed, tx_count, tx_cells)
+    return pl.pallas_call(
+        hand_over_kernel,
+        out_shape=(jax.ShapeDtypeStruct(grad.shape, f32), jax.ShapeDtypeStruct(field.shape, f32)),
+        in_specs=[hbm, hbm],
+        out_specs=(hbm, hbm),
+        scratch_shapes=[
+            pltpu.VMEM(grad.shape, f32),
+            pltpu.VMEM(field.shape[1:], f32),
+            pltpu.SemaphoreType.DMA((2, 8)),
+        ],
+        compiler_params=pltpu.CompilerParams(vmem_limit_bytes=(64 * 1024 - 64) * 1024),
+    )(grad, field)
 
 
 def solution(mesh):

time: 70.8 us -> 62.2 us (0.88)
  Pallas kernels: 64.4 us -> 60.1 us
  local copies, waits for them, and re-layouts: 4.27 us -> 0 us
    pallas_call x1, Pallas kernels: 64.4 us -> 57.8 us  [on_device(): pl.pallas_call(functools.partial(sweeps_kernel, freqs, slabs, tx_max), ou...]
    unnamed x2 -> x0, local copies, waits for them, and re-layouts: 4.27 us -> none
    pallas_call x0 -> x1, Pallas kernels: none -> 2.26 us  [on_device(): pl.pallas_call(hand_over_kernel, out_shape=(jax.ShapeDtypeStruct(grad.sha...]
where the time goes in v4:
time: 62.2 us; the launch traced here: 62 us
  Pallas kernels  60.1 us (97%)
  between operations  1.93 us (3%)
    pallas_call x1, Pallas kernels, on_device(): pl.pallas_call(functools.partial(sweeps_kernel, freqs, slabs, tx_max), ou...  57.8 us
    pallas_call x1, Pallas kernels, on_device(): pl.pallas_call(hand_over_kernel, out_shape=(jax.ShapeDtypeStruct(grad.sha...  2.26 us

profile of v4, /device:TPU:8, one launch (start us, length us, event | category | flops | bytes accessed | tf_op | source)
XLA Modules:
  0.0 62.0 jit_solution(10318729849706436895)
XLA Ops:
  1.9 57.8 %shard_map.95 = (f32[2,4,16,256]{3,2,1,0:T(8,128)}, f32[1,2,3,4,64,256]{5,4,3,2,1,0:T(8,128)}) custom-call(f32[4,64,256]{2,1,0:T(8,128)} %sig_h_in.1, f32[4,64,256]{2,1,0:T(8,128)} %sig_v_in.1, f32[1]{0:T(128)S(6)} %copy.10.wave, bf16[1,2,3,4,64,256]{5,4,3,2,1,0:T(8,128)(2,1)} %field_in.1, bf16[1,2,3,4,64,256]{5,4,3,2,1,0:T(8,128)(2,1)} %adjoint_in.1, ...), custom_call_target="tpu_custom_call" | custom-call | tf_op jit(solution)/shard_map/pallas_call | solution.py:377
  59.7 2.3 %shard_map.96 = (f32[2,4,16,256]{3,2,1,0:T(8,128)}, f32[1,2,3,4,64,256]{5,4,3,2,1,0:T(8,128)}) custom-call(f32[2,4,16,256]{3,2,1,0:T(8,128)} %get-tuple-element.4.grad_in, f32[1,2,3,4,64,256]{5,4,3,2,1,0:T(8,128)} %get-tuple-element.5.field_in), custom_call_target="tpu_custom_call" | custom-call | tf_op jit(solution)/shard_map/pallas_call | solution.py:413

commit v5 on v4

--- a/solution.py
+++ b/solution.py
@@ -208,10 +208,10 @@
         for n, (src, dst) in enumerate((
             (field_in.at[0, :, :, 0], field_start.at[:, :, 0]),
             (field_in.at[0, :, :, last], field_start.at[:, :, last]),
-            (field_in.at[0, :, :, pl.ds(1, last - 1)], field_start.at[:, :, pl.ds(1, last - 1)]),
+            (adjoint_in.at[0], adjoint_start),
             (sig_h_in, sig_h),
             (sig_v_in, sig_v),
-            (adjoint_in.at[0], adjoint_start),
+            (field_in.at[0, :, :, pl.ds(1, last - 1)], field_start.at[:, :, pl.ds(1, last - 1)]),
             (observed_in.at[0], observed),
         ))
     ]
@@ -248,14 +248,15 @@
             yz[s, width] = jnp.zeros((2, 2, rows, cols), jnp.float32)
 
     left_end(E0, whole)
-    for load in loads[2:]:
-        load.wait()
+    loads[2].wait()
     fill(A0, 0, adjoint_start)
     fill(A0, last, adjoint_start)
     for k in range(2):
         send_left(A0, k)
         send_right(A0, k)
     left_end(A0, whole)
+    for load in loads[3:]:
+        load.wait()
 
     def prepare(i):
         for which, sig in enumerate((sig_h, sig_v)):
@@ -321,7 +322,17 @@
         lax.fori_loop(1, last, lambda i, _: (finish_grad(i, 0, i - 1), 0)[1], 0)
     for off in range(1, freqs):
         to_peer(0, off).start()
+    def gather(phase, layers):
+        total = grad_send[phase, me_f]
+        for off in range(1, freqs):
+            to_peer(phase, off).wait_recv()
+            total = total + grad_recv[phase, off]
+        for slot, layer in enumerate(layers):
+            grad_out[:, layer] = total[:, slot]
+
     for k, part in enumerate(((half, rows), (low, half), (0, low))):
+        if k == 2:
+            gather(0, tuple(range(1, last)))
         wait_left(A1, k)
         finish_grad(0, 1, 0, part)
         wait_right(A1, k)
@@ -332,13 +343,7 @@
                 lambda: to_peer(1, off).start()
             )
 
-    for phase, layers in ((0, tuple(range(1, last))), (1, (0, last))):
-        total = grad_send[phase, me_f]
-        for off in range(1, freqs):
-            to_peer(phase, off).wait_recv()
-            total = total + grad_recv[phase, off]
-        for slot, layer in enumerate(layers):
-            grad_out[:, layer] = total[:, slot]
+    gather(1, (0, last))
     store_grad = pltpu.make_async_copy(grad_out, grad_hbm, store_sem.at[1])
     store_grad.start()
     for off in range(1, freqs):

time: 62.2 us -> 62.2 us (level)
  no operation moved by 1% of the time
where the time goes in v5:
time: 62.2 us; the launch traced here: 62 us
  Pallas kernels  60.1 us (97%)
  between operations  1.93 us (3%)
    pallas_call x1, Pallas kernels, on_device(): pl.pallas_call(functools.partial(sweeps_kernel, freqs, slabs, tx_max), ou...  57.8 us
    pallas_call x1, Pallas kernels, on_device(): pl.pallas_call(hand_over_kernel, out_shape=(jax.ShapeDtypeStruct(grad.sha...  2.26 us

profile of v5, /device:TPU:8, one launch (start us, length us, event | category | flops | bytes accessed | tf_op | source)
XLA Modules:
  0.0 62.0 jit_solution(6353216788670629482)
XLA Ops:
  1.9 57.8 %shard_map.95 = (f32[2,4,16,256]{3,2,1,0:T(8,128)}, f32[1,2,3,4,64,256]{5,4,3,2,1,0:T(8,128)}) custom-call(f32[4,64,256]{2,1,0:T(8,128)} %sig_h_in.1, f32[4,64,256]{2,1,0:T(8,128)} %sig_v_in.1, f32[1]{0:T(128)S(6)} %copy.10.wave, bf16[1,2,3,4,64,256]{5,4,3,2,1,0:T(8,128)(2,1)} %field_in.1, bf16[1,2,3,4,64,256]{5,4,3,2,1,0:T(8,128)(2,1)} %adjoint_in.1, ...), custom_call_target="tpu_custom_call" | custom-call | tf_op jit(solution)/shard_map/pallas_call | solution.py:382
  59.7 2.3 %shard_map.96 = (f32[2,4,16,256]{3,2,1,0:T(8,128)}, f32[1,2,3,4,64,256]{5,4,3,2,1,0:T(8,128)}) custom-call(f32[2,4,16,256]{3,2,1,0:T(8,128)} %get-tuple-element.4.grad_in, f32[1,2,3,4,64,256]{5,4,3,2,1,0:T(8,128)} %get-tuple-element.5.field_in), custom_call_target="tpu_custom_call" | custom-call | tf_op jit(solution)/shard_map/pallas_call | solution.py:418
